TPU v7x, 32 devices: a whole 2x2x4 slice. The times are simulated.
32 devices in a mesh: ctx: 4 (over x, core), tp: 8 (over z, y).
Axes of the slice: x: 2, y: 2, z: 4, core: 2. Of those that a mesh axis runs over, the one named last changes fastest.
Arguments:
- query_feats: bfloat16 [8192, 512], P('tp', 'ctx'), may hold values from -6 to 6
- key_feats: bfloat16 [8192, 512], P('tp', 'ctx'), may hold values from -6 to 6
- value_feats: bfloat16 [8192, 512], P('tp', 'ctx'), may hold values from -6 to 6
- out_gate: bfloat16 [8192, 512], P('tp', 'ctx'), may hold values from -6 to 6
- mr_filter: bfloat16 [512, 128], P('tp'), may hold values from -0.5 to 0.5
- lr_rates: float32 [512, 16], P('tp'), may hold values from 0.0009765625 to 0.1
- lr_residues: float32 [512, 16], P('tp'), may hold values from -6 to 6
- w_out: bfloat16 [8192, 8192], P('tp'), may hold values from -0.09375 to 0.09375
Outputs:
- mixed_out: bfloat16 [8192, 512], P('tp', 'ctx')
All inputs are finite; a program needn't handle non-finite values.
Results may differ from a plain program's by a relative error of at most 0.023.
Values may be sent and summed in bfloat16 or wider, within the bound.
A program may use at most 128 MiB of HBM per device.

v0:
```python
import jax
import jax.numpy as jnp
from jax import lax
from jax.sharding import PartitionSpec as P

chan_group = 16


def passed_along(value, axis, steps):
    count = lax.axis_size(axis)
    first, last = (max(0, -steps), min(count, count - steps))
    return lax.ppermute(value, axis, [(source, source + steps) for source in range(first, last)])


def entering(value, axis, join, neutral):
    place = lax.axis_index(axis)
    gathered = jax.tree.map(
        lambda a, kind: lax.all_gather(a.astype(kind), axis), value, (jnp.bfloat16, jnp.bfloat16)
    )
    state = jax.tree.map(lambda a, e: jnp.zeros_like(a) + jnp.asarray(e, a.dtype), value, neutral)

    def one(lap, state):
        return join(
            state,
            jax.tree.map(
                lambda a, own: lax.dynamic_index_in_dim(a, lap, 0, False).astype(own.dtype),
                gathered,
                value,
            ),
        )

    return lax.fori_loop(0, place, one, state)


def lr_filter(decay_rates, residues_in, length):
    positions = jnp.arange(length).astype(jnp.float32)
    decays = jnp.exp(-decay_rates[:, :, None] * positions[None, None, :])
    weights = residues_in * jnp.sqrt(2.0 * decay_rates / decay_rates.shape[1])
    return jnp.sum(weights[:, :, None] * decays, axis=1)


def skew(vector, row_count, col_count):
    lead = vector.shape[0]
    full_len = row_count + col_count
    padded = jnp.concatenate([vector, jnp.zeros((lead, 1), vector.dtype)], axis=1)
    rolled = jnp.concatenate([padded[:, row_count - 1 :], padded[:, : row_count - 1]], axis=1)
    tiled = jnp.broadcast_to(rolled[:, None, :], (lead, row_count, full_len)).reshape(
        lead, row_count * full_len
    )
    shaped = tiled[:, : row_count * (full_len - 1)].reshape(lead, row_count, full_len - 1)
    return shaped[:, :, :col_count]


def medium_tokens(rim_rows, kv_prod, query_feats, mr_filter):
    channels, tokens_here = kv_prod.shape
    rim_len = rim_rows.shape[1]
    local_groups = mr_filter.shape[0]
    extended = jnp.concatenate([rim_rows, kv_prod], axis=1)
    span = tokens_here + rim_len
    padded_taps = jnp.concatenate(
        [
            jnp.zeros((local_groups, span), jnp.bfloat16),
            mr_filter,
            jnp.zeros((local_groups, span), jnp.bfloat16),
        ],
        axis=1,
    )
    vector = padded_taps[:, rim_len + 1 : rim_len + span + tokens_here]
    toeplitz = skew(vector, span, tokens_here)
    medium = jnp.einsum(
        "gcs,gst->gct",
        extended.reshape(local_groups, chan_group, span),
        toeplitz,
        preferred_element_type=jnp.float32,
    )
    return (query_feats.astype(jnp.float32) * medium.reshape(channels, tokens_here)).astype(
        jnp.bfloat16
    )


def modal_parts(signal, decay_rates, residues_in):
    group_count, group_chans, length = signal.shape
    taps_here = lr_filter(decay_rates, residues_in, length)
    padded = jnp.concatenate([jnp.zeros((group_count, length), jnp.float32), taps_here], axis=1)
    toeplitz = skew(padded[:, 1:], length, length)
    signal_wide = signal.astype(jnp.float32)
    local_part = jnp.einsum("gcs,gst->gct", signal_wide, toeplitz, precision=lax.Precision.HIGHEST)
    positions = jnp.arange(length).astype(jnp.float32)
    tail = jnp.exp(-decay_rates[:, None, :] * (length - 1.0 - positions)[None, :, None])
    states = jnp.einsum("gcs,gsn->gcn", signal_wide, tail, precision=lax.Precision.HIGHEST)
    step_decay = jnp.broadcast_to(jnp.exp(-decay_rates * length)[:, None, :], states.shape)
    weights = residues_in * jnp.sqrt(2.0 * decay_rates / decay_rates.shape[1])
    coeffs = weights[:, :, None] * jnp.exp(
        -decay_rates[:, :, None] * (positions + 1.0)[None, None, :]
    )
    return (local_part, states, step_decay, coeffs)


def join_modes(earlier, later):
    return (earlier[0] * later[0], earlier[1] * later[0] + later[1])


def per_device(
    query_feats, key_feats, value_feats, out_gate, mr_filter, lr_rates, lr_residues, w_out
):
    channels, tokens_here = key_feats.shape
    rim_len = mr_filter.shape[1] - 1
    kv_prod = (key_feats.astype(jnp.float32) * value_feats.astype(jnp.float32)).astype(jnp.bfloat16)
    rim_rows = passed_along(kv_prod[:, tokens_here - rim_len :], "ctx", 1)
    gated_mid = medium_tokens(rim_rows, kv_prod, query_feats, mr_filter)
    local_groups = mr_filter.shape[0]
    local_part, states, step_decay, coeffs = modal_parts(
        gated_mid.reshape(local_groups, chan_group, tokens_here), lr_rates, lr_residues
    )
    carried = entering(
        (step_decay, states), "ctx", join_modes, (jnp.ones_like(step_decay), jnp.zeros_like(states))
    )
    long_wide = local_part + jnp.einsum(
        "gcn,gnt->gct", carried[1], coeffs, precision=lax.Precision.HIGHEST
    )
    returned = long_wide.reshape(channels, tokens_here).astype(jnp.bfloat16)
    gated_out = (out_gate.astype(jnp.float32) * returned.astype(jnp.float32)).astype(jnp.bfloat16)
    return lax.psum_scatter(
        lax.dot_general(
            w_out, gated_out, (((0,), (0,)), ((), ())), preferred_element_type=jnp.float32
        ).astype(jnp.bfloat16),
        "tp",
        scatter_dimension=0,
        tiled=True,
    )


def solution(mesh):
    placed = (
        P("tp", "ctx"),
        P("tp", "ctx"),
        P("tp", "ctx"),
        P("tp", "ctx"),
        P("tp", None),
        P("tp", None),
        P("tp", None),
        P("tp", None),
    )
    return jax.shard_map(
        per_device, mesh=mesh, in_specs=placed, out_specs=P("tp", "ctx"), check_vma=False
    )
```

profile of v0, /device:TPU:26, one launch (start us, length us, event | category | flops | bytes accessed | tf_op | source)
XLA Modules:
  0.0 221.2 jit_solution(12108778067322827877)
XLA Ops:
  6.5 1.1 multiply_convert_fusion
  7.8 1.9 collective-permute-start
  9.7 0.8 pad_slice_fusion.2
  10.5 0.8 fusion.23
  11.3 0.7 fusion.24
  12.2 0.3 multiply_reduce_fusion
  12.8 5.6 %broadcast_in_dim.6 = bf16[64,255,383]{2,1,0:T(8,128)(2,1)} broadcast(bf16[64,383]{1,0:T(8,128)(2,1)S(1)} %pad_maximum_fusion.1), dimensions={0,2} | broadcast | bytes 12550144 | tf_op jit(solution)/shard_map/broadcast_in_dim | solution.py:47
  18.4 20.5 %reshape.50 = bf16[64,97665]{1,0:T(8,128)(2,1)} reshape(bf16[64,255,383]{2,1,0:T(8,128)(2,1)} %broadcast_in_dim.6) | data formatting | bytes 25002240 | tf_op jit(solution)/shard_map/reshape | solution.py:47
  38.9 10.4 %slice.45 = bf16[64,97410]{1,0:T(8,128)(2,1)} slice(bf16[64,97665]{1,0:T(8,128)(2,1)} %reshape.50), slice={[0:64], [0:97410]} | slice | bytes 24936960 | tf_op jit(solution)/shard_map/slice | solution.py:50
  49.3 35.4 %reshape.51 = bf16[64,255,382]{2,1,0:T(8,128)(2,1)} reshape(bf16[64,97410]{1,0:T(8,128)(2,1)} %slice.45) | data formatting | bytes 24936960 | tf_op jit(solution)/shard_map/reshape | solution.py:50
  84.7 0.7 broadcast_in_dim.7
  85.4 4.7 %copy.27 = f32[8,8,128,256]{3,1,2,0:T(8,128)S(1)} copy(f32[8,8,128,256]{3,2,1,0:T(8,128)S(1)} %bitcast.30) | data formatting | bytes 16777216
  90.1 3.8 %slice.47 = f32[64,32640]{1,0:T(8,128)} slice(f32[64,32768]{1,0:T(8,128)S(1)} %bitcast.31), slice={[0:64], [0:32640]} | slice | bytes 16711680 | tf_op jit(solution)/shard_map/slice | solution.py:50
  94.0 15.9 %reshape.55 = f32[64,128,255]{2,1,0:T(8,128)} reshape(f32[64,32640]{1,0:T(8,128)} %slice.47) | data formatting | bytes 16711680 | tf_op jit(solution)/shard_map/reshape | solution.py:50
  109.9 5.2 %all-gather.2 = bf16[4,64,16]{1,2,0:T(8,128)(2,1)S(1)} all-gather(bf16[1,64,16]{1,2,0:T(8,128)(2,1)S(1)} %get-tuple-element.75), channel_id=3, replica_groups=mesh['ctx'=4,'tp'=8] {'ctx'}, dimensions={0}, use_global_device_ids=true | all-gather | bytes 10240 | tf_op jit(solution)/shard_map/all_gather | solution.py:18
  115.4 2.9 %fusion.3 = f32[64,16,128]{2,1,0:T(8,128)S(1)} fusion(bf16[64,16,255]{2,1,0:T(8,128)(2,1)S(1)} %bitcast.33, bf16[64,255,382]{2,1,0:T(8,128)(2,1)} %reshape.51), kind=kOutput, calls=%fused_computation.6 | convolution fusion | flops 66846720 | bytes 5240832 | tf_op jit(solution)/shard_map/gcs,gst->gct/dot_general | solution.py:70
  118.4 3.7 %fusion.1 = f32[64,16,128]{2,1,0:T(8,128)S(1)} fusion(bf16[64,16,128]{2,1,0:T(8,128)(2,1)S(1)} %bitcast.35, f32[64,128,255]{2,1,0:T(8,128)} %reshape.55), kind=kOutput, calls=%fused_computation.4 | convolution fusion | flops 201326592 | bytes 4980736 | tf_op jit(solution)/shard_map/gcs,gst->gct/dot_general | solution.py:87
  122.1 0.6 convolution_convert_fusion.1
  122.8 10.1 %all-gather.1 = bf16[256,16,16]{2,1,0:T(8,128)(2,1)S(1)} all-gather(bf16[64,16,16]{2,1,0:T(8,128)(2,1)S(1)} %convolution_convert_fusion.1), channel_id=4, replica_groups=mesh['ctx'=4,'tp'=8] {'ctx'}, dimensions={0}, use_global_device_ids=true | all-gather | bytes 163840 | tf_op jit(solution)/shard_map/all_gather | solution.py:18
  132.9 0.8 copy.24
  134.2 0.8 fusion.5
  135.0 9.6 %fusion = bf16[8192,128]{0,1:T(8,128)(2,1)} fusion(bf16[1024,8192]{1,0:T(8,128)(2,1)} %param.17, bf16[1024,128]{1,0:T(8,128)(2,1)S(1)} %bitcast.34, bf16[1024,128]{1,0:T(8,128)(2,1)S(1)} %copy-done), kind=kOutput, calls=%fused_computation.3 | convolution fusion | flops 2149056512 | bytes 19398656 | tf_op jit(solution)/shard_map/dot_general | solution.py:124
  144.6 68.0 %reduce-scatter.2.cloned.1.call-done = bf16[1024,128]{0,1:T(8,128)(2,1)} async-done(((bf16[8192,128]{0,1:T(8,128)(2,1)}), bf16[1024,128]{0,1:T(8,128)(2,1)}) %reduce-scatter.2.cloned.1.call-update) | async-done | bytes 262160 | tf_op jit(solution)/shard_map/reduce_scatter | solution.py:123
  212.6 1.8 copy.26
  (26 shorter events, 1.5 us)
Async XLA Ops:
  6.5 206.1 %reduce-scatter.2.cloned.1.call-start = ((), (), s32[]{:S(2)}) async-start(), calls=%async_computation.1 | async-start | bytes 2359296 | tf_op jit(solution)/shard_map/reduce_scatter | solution.py:123
  7.8 107.4 %collective-permute-start = (bf16[1024,127]{1,0:T(8,128)(2,1)S(1)}, bf16[1024,127]{1,0:T(8,128)(2,1)S(1)}, u32[]{:S(2)}, u32[]{:S(2)}) collective-permute-start(bf16[1024,127]{1,0:T(8,128)(2,1)S(1)} %slice.44), channel_id=1, source_target_pairs={{0,8},{8,16},{16,24},{1,9},{9,17},{17,25},{2,10},{10,18},{18,26},{... | collective-permute-start | bytes 780296 | tf_op jit(solution)/shard_map/ppermute | solution.py:12
  94.0 24.3 %copy-start.1 = (bf16[1024,128]{1,0:T(8,128)(2,1)S(1)}, bf16[1024,128]{1,0:T(8,128)(2,1)}, u32[]{:S(2)}) copy-start(bf16[1024,128]{1,0:T(8,128)(2,1)} %param.10) | copy-start | bytes 786436
  115.4 19.6 %copy-start = (bf16[1024,128]{1,0:T(8,128)(2,1)S(1)}, bf16[1024,128]{1,0:T(8,128)(2,1)}, u32[]{:S(2)}) copy-start(bf16[1024,128]{1,0:T(8,128)(2,1)} %param.13) | copy-start | bytes 786436
Sparse Core Ops, SparseCore 0:
  144.8 67.7 reduce-scatter.1
where the time goes:
time: 225 us; the launch traced here: 221 us
  local copies, waits for them, and re-layouts  101 us (45%)
  waiting for transfers between devices  68 us (30%)
  matrix products  17.6 us (8%)
  blocking collectives  15.3 us (7%)
  between operations  13.6 us (6%)
  other arithmetic  3.49 us (2%)
    reduce_scatter x1, waiting for transfers between devices, per_device(): lax.psum_scatter(lax.dot_general(w_out, gated_out, (((0,), (0,)), ((), ()...  68 us
    reshape x2, local copies, waits for them, and re-layouts, skew(): tiled[:, :row_count * (full_len - 1)].reshape(lead, row_count, full_len - 1)  51.4 us
    reshape x1, local copies, waits for them, and re-layouts, skew(): jnp.broadcast_to(rolled[:, None, :], (lead, row_count, full_len))  20.5 us
    all_gather x2, blocking collectives, entering(): lax.all_gather(a.astype(kind), axis)  15.3 us
    slice x2, local copies, waits for them, and re-layouts, skew(): tiled[:, :row_count * (full_len - 1)].reshape(lead, row_count, full_len - 1)  14.2 us
    dot_general x1, matrix products, per_device(): lax.dot_general(w_out, gated_out, (((0,), (0,)), ((), ())), preferred_ele...  9.58 us
    broadcast_in_dim x2, local copies, waits for them, and re-layouts, skew(): jnp.broadcast_to(rolled[:, None, :], (lead, row_count, full_len))  6.22 us
    unnamed x6, local copies, waits for them, and re-layouts  4.78 us
  transfers between devices with their start and end apart: 2, of which 1 were waited for; matrix products, arithmetic and copies ran while one was open for 45% of the time, Pallas kernels for 0%

commit v1 on v0

v1 whole, which is shorter than its diff:
```python
import functools

import jax
import jax.numpy as jnp
from jax import lax
from jax.experimental import pallas as pl
from jax.experimental.pallas import tpu as pltpu
from jax.sharding import PartitionSpec as P

chan_group = 16
MESH = pl.DeviceIdType.MESH
HIGH = lax.Precision.HIGHEST


def dot(a, b, dims=((1,), (0,)), precision=None):
    return lax.dot_general(
        a, b, (dims, ((), ())), preferred_element_type=jnp.float32, precision=precision
    )


def iota(shape, dim):
    return lax.broadcasted_iota(jnp.int32, shape, dim)


def kernel(
    n_ctx,
    n_tp,
    q_ref,
    k_ref,
    v_ref,
    og_ref,
    mr_ref,
    rates_ref,
    res_ref,
    w_hbm,
    out_ref,
    w_ref,
    kv_ref,
    halo_ref,
    gm_ref,
    gt_ref,
    mrf_ref,
    rrow_ref,
    wrow_ref,
    med_ref,
    lng_ref,
    tail_ref,
    coef_ref,
    loc_ref,
    pack_ref,
    packf_ref,
    slot_ref,
    ysend,
    yrecv,
    acc,
    zsend,
    zrecv,
    w_sem,
    halo_send,
    halo_recv,
    st_send,
    st_recv,
    ys_sem,
    yr_sem,
    zs_sem,
    zr_sem,
):
    channels, tokens = q_ref.shape
    order = rates_ref.shape[1]
    groups = mr_ref.shape[0]
    per = tokens // order
    blocks = groups // per
    span = per * chan_group
    e_block = out_ref.shape[0]
    cw = ysend.shape[3]
    chunks = e_block // cw
    n_z = n_tp // 2
    i = lax.axis_index("ctx")
    me = lax.axis_index("tp")
    z = me // 2
    y = me % 2

    def target(p):
        q = n_z - 1 - p
        low = q - jnp.where(q <= z, 1, 0)
        high = p + jnp.where(p >= z, 1, 0)
        return jnp.where(p == n_z - 1, z, jnp.where(z < n_z // 2, low, high))

    def w_copy(b):
        cols = pl.ds(pl.multiple_of(b * e_block, e_block), e_block)
        return pltpu.make_async_copy(w_hbm.at[:, cols], w_ref.at[b], w_sem.at[b])

    @pl.loop(0, n_tp)
    def _(b):
        w_copy(b).start()

    barrier = pltpu.get_barrier_semaphore()
    for d in range(1, n_ctx):
        pl.semaphore_signal(
            barrier, inc=1, device_id={"ctx": lax.rem(i + d, n_ctx)}, device_id_type=MESH
        )
    pl.semaphore_signal(
        barrier, inc=1, device_id={"tp": z * 2 + 1 - y}, device_id_type=MESH
    )

    @pl.when(z > 0)
    def _():
        pl.semaphore_signal(barrier, inc=1, device_id={"tp": me - 2}, device_id_type=MESH)

    @pl.when(z < n_z - 1)
    def _():
        pl.semaphore_signal(barrier, inc=1, device_id={"tp": me + 2}, device_id_type=MESH)

    kv_ref[...] = (
        k_ref[...].astype(jnp.float32) * v_ref[...].astype(jnp.float32)
    ).astype(jnp.bfloat16)

    pl.semaphore_wait(
        barrier, n_ctx + jnp.where(z > 0, 1, 0) + jnp.where(z < n_z - 1, 1, 0)
    )

    halo_copy = pltpu.make_async_remote_copy(
        src_ref=kv_ref,
        dst_ref=halo_ref,
        send_sem=halo_send,
        recv_sem=halo_recv,
        device_id={"ctx": lax.rem(i + 1, n_ctx)},
        device_id_type=MESH,
    )

    @pl.when(i < n_ctx - 1)
    def _():
        halo_copy.start()

    @pl.when(i == 0)
    def _():
        halo_ref[...] = jnp.zeros_like(halo_ref)

    mrf_ref[...] = mr_ref[...].astype(jnp.float32)
    rates = rates_ref[...]
    weights = res_ref[...] * jnp.sqrt(2.0 * rates / order)
    own = iota((groups, tokens), 1) // order == iota((groups, tokens), 0) % per
    for src, dst in ((rates, rrow_ref), (weights, wrow_ref)):
        wide = jnp.where(own, jnp.concatenate([src] * per, axis=1), 0.0)
        dst[...] = jnp.sum(wide.reshape(blocks, per, tokens), axis=1)

    square = (tokens, tokens)
    row_i, col_i = iota(square, 0), iota(square, 1)
    same = row_i // chan_group == col_i // order

    @pl.loop(0, blocks)
    def _(k):
        r = rrow_ref[pl.ds(k, 1), :]
        place = row_i.astype(jnp.float32)
        exp0 = jnp.exp(-r * place)
        tail_ref[k] = jnp.exp(-r * (tokens - 1.0 - place))
        coef_ref[k] = exp0 * jnp.exp(-r)
        w_sel = jnp.where(
            iota((per, tokens), 1) // order == iota((per, tokens), 0),
            wrow_ref[pl.ds(k, 1), :],
            0.0,
        )
        taps = dot(w_sel, exp0, ((1,), (1,)), HIGH)
        mr = mrf_ref[pl.ds(pl.multiple_of(k * per, per), per), :]
        for g in range(per):
            circ = pltpu.roll(
                jnp.broadcast_to(taps[g : g + 1, :], square), 0, 1, stride=1, stride_axis=0
            )
            lng_ref[k * per + g] = jnp.where(row_i <= col_i, circ, 0.0).astype(jnp.bfloat16)
            circ = pltpu.roll(
                jnp.broadcast_to(mr[g : g + 1, :], square), 0, 1, stride=1, stride_axis=0
            )
            med_ref[k * per + g, :tokens, :] = jnp.where(row_i > col_i, circ, 0.0).astype(
                jnp.bfloat16
            )
            med_ref[k * per + g, tokens:, :] = jnp.where(row_i <= col_i, circ, 0.0).astype(
                jnp.bfloat16
            )

    packf_ref[...] = jnp.zeros_like(packf_ref)

    @pl.when(i > 0)
    def _():
        halo_copy.wait_recv()

    @pl.loop(0, blocks)
    def _(k):
        for g in range(per):
            rows = pl.ds(pl.multiple_of((k * per + g) * chan_group, chan_group), chan_group)
            signal = jnp.concatenate([halo_ref[rows, :], kv_ref[rows, :]], axis=1)
            medium = dot(signal, med_ref[k * per + g])
            gm_ref[rows, :] = (q_ref[rows, :].astype(jnp.float32) * medium).astype(jnp.bfloat16)
        rows = pl.ds(pl.multiple_of(k * span, span), span)
        state = dot(gm_ref[rows, :].astype(jnp.float32), tail_ref[k], precision=HIGH)
        state = jnp.where(same, state, 0.0).astype(jnp.bfloat16)
        spread = jnp.where(col_i == k * order + row_i % order, 1.0, 0.0).astype(jnp.bfloat16)
        packf_ref[...] += dot(state, spread)

    pack_ref[...] = packf_ref[...].astype(jnp.bfloat16)

    def st_copy(d):
        return pltpu.make_async_remote_copy(
            src_ref=pack_ref,
            dst_ref=slot_ref.at[d],
            send_sem=st_send.at[d],
            recv_sem=st_recv.at[d],
            device_id={"ctx": lax.rem(i + d + 1, n_ctx)},
            device_id_type=MESH,
        )

    @pl.loop(0, n_ctx - 1)
    def _(d):
        @pl.when(i + d + 1 < n_ctx)
        def _():
            st_copy(d).start()

        @pl.when(i < d + 1)
        def _():
            slot_ref[d] = jnp.zeros(square, jnp.bfloat16)

    @pl.loop(0, blocks)
    def _(k):
        for g in range(per):
            rows = pl.ds(pl.multiple_of((k * per + g) * chan_group, chan_group), chan_group)
            loc_ref[rows, :] = dot(gm_ref[rows, :], lng_ref[k * per + g])

    @pl.loop(0, n_ctx - 1)
    def _(d):
        @pl.when(i >= d + 1)
        def _():
            st_copy(d).wait_recv()

    @pl.loop(0, blocks)
    def _(k):
        rows = pl.ds(pl.multiple_of(k * span, span), span)
        r = rrow_ref[pl.ds(k, 1), :]
        gather = jnp.where(row_i == k * order + col_i % order, 1.0, 0.0).astype(jnp.bfloat16)

        def add(d, total):
            fade = jnp.exp(-r * (tokens * d).astype(jnp.float32))
            return total + fade * dot(slot_ref[d], gather)

        carried = lax.fori_loop(0, n_ctx - 1, add, jnp.zeros(square, jnp.float32))
        carried = jnp.where(same, carried * wrow_ref[pl.ds(k, 1), :], 0.0)
        wide = loc_ref[rows, :] + dot(carried, coef_ref[k], ((1,), (1,)), HIGH)
        gated = og_ref[rows, :].astype(jnp.float32) * wide.astype(jnp.bfloat16).astype(jnp.float32)
        gt_ref[:, rows] = gated.T.astype(jnp.bfloat16)

    @pl.loop(0, n_tp)
    def _(b):
        w_copy(b).wait()

    def y_copy(p, c):
        return pltpu.make_async_remote_copy(
            src_ref=ysend.at[p, c],
            dst_ref=yrecv.at[p, c],
            send_sem=ys_sem.at[p, c],
            recv_sem=yr_sem.at[p, c],
            device_id={"tp": z * 2 + 1 - y},
            device_id_type=MESH,
        )

    def z_copy(p, c):
        zt = target(p)
        back = jnp.where(zt < z, 1, 0)
        return pltpu.make_async_remote_copy(
            src_ref=zsend.at[p, c],
            dst_ref=zrecv.at[back, zt, c],
            send_sem=zs_sem.at[p, c],
            recv_sem=zr_sem.at[back, zt, c],
            device_id={"tp": lax.rem(me + 2 - 4 * back + n_tp, n_tp)},
            device_id_type=MESH,
        )

    def z_wait(way, zt, c):
        pltpu.make_async_remote_copy(
            src_ref=zsend.at[0, c],
            dst_ref=zrecv.at[way, zt, c],
            send_sem=zs_sem.at[0, c],
            recv_sem=zr_sem.at[way, zt, c],
            device_id={"tp": z * 2 + 1 - y},
            device_id_type=MESH,
        ).wait_recv()

    @pl.loop(0, n_z)
    def _(p):
        b = target(p) * 2 + 1 - y
        for c in range(chunks):
            ysend[p, c] = dot(gt_ref[...], w_ref[b, :, c * cw : (c + 1) * cw]).astype(jnp.bfloat16)
            y_copy(p, c).start()

    @pl.loop(0, n_z)
    def _(p):
        b = target(p) * 2 + y
        for c in range(chunks):
            acc[p, c] = dot(gt_ref[...], w_ref[b, :, c * cw : (c + 1) * cw])

    @pl.loop(0, n_z - 1)
    def _(p):
        zt = target(p)
        back = jnp.where(zt < z, 1, 0)
        joins = jnp.where(zt < z, z < n_z - 1, z > 0)

        @pl.loop(0, chunks)
        def _(c):
            y_copy(p, c).wait_recv()
            acc[p, c] += yrecv[p, c].astype(jnp.float32)

            @pl.when(joins)
            def _():
                z_wait(back, zt, c)
                acc[p, c] += zrecv[back, zt, c].astype(jnp.float32)

            zsend[p, c] = acc[p, c].astype(jnp.bfloat16)
            z_copy(p, c).start()

    for c in range(chunks):
        y_copy(n_z - 1, c).wait_recv()
        acc[n_z - 1, c] += yrecv[n_z - 1, c].astype(jnp.float32)

        @pl.when(z > 0)
        def _():
            z_wait(0, z, c)
            acc[n_z - 1, c] += zrecv[0, z, c].astype(jnp.float32)

        @pl.when(z < n_z - 1)
        def _():
            z_wait(1, z, c)
            acc[n_z - 1, c] += zrecv[1, z, c].astype(jnp.float32)

        out_ref[c * cw : (c + 1) * cw, :] = acc[n_z - 1, c].T.astype(jnp.bfloat16)

    @pl.when(i < n_ctx - 1)
    def _():
        halo_copy.wait_send()

    @pl.loop(0, n_ctx - 1)
    def _(d):
        @pl.when(i + d + 1 < n_ctx)
        def _():
            st_copy(d).wait_send()

    @pl.loop(0, n_z)
    def _(p):
        for c in range(chunks):
            y_copy(p, c).wait_send()

    @pl.loop(0, n_z - 1)
    def _(p):
        for c in range(chunks):
            z_copy(p, c).wait_send()


def per_device(n_ctx, n_tp, q, k, v, og, mr, rates, res, w):
    channels, tokens = q.shape
    groups, order = rates.shape
    assert tokens == mr.shape[1] and tokens % order == 0 and n_tp % 2 == 0
    blocks = groups * order // tokens
    e_block = w.shape[1] // n_tp
    cw = min(e_block, 256)
    chunks = e_block // cw
    n_z = n_tp // 2
    bf, f32 = jnp.bfloat16, jnp.float32
    dma = pltpu.SemaphoreType.DMA
    vmem = pl.BlockSpec(memory_space=pltpu.VMEM)
    return pl.pallas_call(
        functools.partial(kernel, n_ctx, n_tp),
        out_shape=jax.ShapeDtypeStruct((e_block, tokens), bf),
        in_specs=[vmem] * 7 + [pl.BlockSpec(memory_space=pl.ANY)],
        out_specs=vmem,
        scratch_shapes=[
            pltpu.VMEM((n_tp, channels, e_block), bf),
            pltpu.VMEM((channels, tokens), bf),
            pltpu.VMEM((channels, tokens), bf),
            pltpu.VMEM((channels, tokens), bf),
            pltpu.VMEM((tokens, channels), bf),
            pltpu.VMEM((groups, tokens), f32),
            pltpu.VMEM((blocks, tokens), f32),
            pltpu.VMEM((blocks, tokens), f32),
            pltpu.VMEM((groups, 2 * tokens, tokens), bf),
            pltpu.VMEM((groups, tokens, tokens), bf),
            pltpu.VMEM((blocks, tokens, tokens), f32),
            pltpu.VMEM((blocks, tokens, tokens), f32),
            pltpu.VMEM((channels, tokens), f32),
            pltpu.VMEM((tokens, tokens), bf),
            pltpu.VMEM((tokens, tokens), f32),
            pltpu.VMEM((n_ctx - 1, tokens, tokens), bf),
            pltpu.VMEM((n_z, chunks, tokens, cw), bf),
            pltpu.VMEM((n_z, chunks, tokens, cw), bf),
            pltpu.VMEM((n_z, chunks, tokens, cw), f32),
            pltpu.VMEM((n_z, chunks, tokens, cw), bf),
            pltpu.VMEM((2, n_z, chunks, tokens, cw), bf),
            dma((n_tp,)),
            dma,
            dma,
            dma((n_ctx - 1,)),
            dma((n_ctx - 1,)),
            dma((n_z, chunks)),
            dma((n_z, chunks)),
            dma((n_z, chunks)),
            dma((2, n_z, chunks)),
        ],
        compiler_params=pltpu.CompilerParams(
            collective_id=0, has_side_effects=True, vmem_limit_bytes=56 * 2**20
        ),
        name="conv_project",
    )(q, k, v, og, mr, rates, res, w)


def solution(mesh):
    placed = (
        P("tp", "ctx"),
        P("tp", "ctx"),
        P("tp", "ctx"),
        P("tp", "ctx"),
        P("tp", None),
        P("tp", None),
        P("tp", None),
        P("tp", None),
    )
    return jax.shard_map(
        functools.partial(per_device, mesh.shape["ctx"], mesh.shape["tp"]),
        mesh=mesh,
        in_specs=placed,
        out_specs=P("tp", "ctx"),
        check_vma=False,
    )
```

time: 225 us -> 53.4 us (0.24); the launches traced: 221 us -> 52.9 us
  local copies, waits for them, and re-layouts: 101 us -> 4.44 us
  waiting for transfers between devices: 68 us -> 0 us
  Pallas kernels: 0 us -> 48.5 us
  matrix products: 17.6 us -> 0 us
  blocking collectives: 15.3 us -> 0 us
  between operations: 13.6 us -> 0.01 us
  other arithmetic: 3.49 us -> 0 us
    reshape x3 -> x0, local copies, waits for them, and re-layouts: 71.9 us -> none  [the longest x2 51.4 us: skew(): tiled[:, :row_count * (full_len - 1)].reshape(lead, row_count, full_len - 1)]
    reduce_scatter x1 -> x0, waiting for transfers between devices: 68 us -> none  [per_device(): lax.psum_scatter(lax.dot_general(w_out, gated_out, (((0,), (0,)), ((), ()...]
    pallas_call x0 -> x1, Pallas kernels: none -> 48.5 us  [per_device(): pl.pallas_call(functools.partial(kernel, n_ctx, n_tp), out_shape=jax.Shap...]
    dot_general x5 -> x0, matrix products: 17.6 us -> none  [the longest x1 9.58 us: per_device(): lax.dot_general(w_out, gated_out, (((0,), (0,)), ((), ())), preferred_ele...]
    all_gather x2 -> x0, blocking collectives: 15.3 us -> none  [entering(): lax.all_gather(a.astype(kind), axis)]
    slice x6 -> x0, local copies, waits for them, and re-layouts: 15.3 us -> none  [the longest x2 14.2 us: skew(): tiled[:, :row_count * (full_len - 1)].reshape(lead, row_count, full_len - 1)]
    broadcast_in_dim x3 -> x0, local copies, waits for them, and re-layouts: 6.23 us -> none  [the longest x2 6.22 us: skew(): jnp.broadcast_to(rolled[:, None, :], (lead, row_count, full_len))]
    unnamed x6 -> x3, local copies, waits for them, and re-layouts: 4.78 us -> 4.44 us
  transfers between devices with their start and end apart: 2 -> 0, of which waited for: 1 -> 0; matrix products, arithmetic and copies ran while one was open for 45% -> 0% of each run, Pallas kernels for 0% -> 0%
where the time goes in v1:
time: 53.4 us; the launch traced here: 52.9 us
  Pallas kernels  48.5 us (91%)
  local copies, waits for them, and re-layouts  4.44 us (8%)
    pallas_call x1, Pallas kernels, per_device(): pl.pallas_call(functools.partial(kernel, n_ctx, n_tp), out_shape=jax.Shap...  48.5 us
    unnamed x3, local copies, waits for them, and re-layouts  4.44 us

profile of v1, /device:TPU:26, one launch (start us, length us, event | category | flops | bytes accessed | tf_op | source)
XLA Modules:
  0.0 52.9 jit_solution(17256532770518845562)
XLA Ops:
  0.0 1.4 %copy.9.rates_ref = f32[64,16]{1,0:T(8,128)} copy(f32[64,16]{0,1:T(8,128)} %param.13) | data formatting | bytes 8192 | tf_op args[5]
  1.4 1.4 %copy.10.res_ref = f32[64,16]{1,0:T(8,128)} copy(f32[64,16]{0,1:T(8,128)} %param.14) | data formatting | bytes 8192 | tf_op args[6]
  2.8 48.5 %conv_project.1 = bf16[1024,128]{1,0:T(8,128)(2,1)} custom-call(bf16[1024,128]{1,0:T(8,128)(2,1)} %q_ref.1, bf16[1024,128]{1,0:T(8,128)(2,1)} %k_ref.1, bf16[1024,128]{1,0:T(8,128)(2,1)} %v_ref.1, bf16[1024,128]{1,0:T(8,128)(2,1)} %og_ref.1, bf16[64,128]{1,0:T(8,128)(2,1)} %mr_ref.1, f32[64,16]{1,0:T(8,128)} %copy.9.rates_ref, f32[64,16]{1,0:T(8,128)} %copy.10.res_ref, ...), custom_call_target="tpu_custom_call" | custom-call | tf_op jit(solution)/shard_map/conv_project/pallas_call | solution.py:366
  51.3 1.7 %copy.12 = bf16[1024,128]{1,0:T(8,128)(2,1)} copy(bf16[1024,128]{1,0:T(8,128)(2,1)} %conv_project.1) | data formatting | bytes 524288

commit v2 on v1

--- a/solution.py
+++ b/solution.py
@@ -16,6 +16,18 @@
     return lax.dot_general(
         a, b, (dims, ((), ())), preferred_element_type=jnp.float32, precision=precision
     )
+
+
+def upright(a, size):
+    rows, cols = a.shape
+    a = jnp.concatenate([a, jnp.zeros((size - rows, cols), a.dtype)], axis=0)
+    a = jnp.concatenate([a, jnp.zeros((size, size - cols), a.dtype)], axis=1)
+    return a.T[:cols, :rows]
+
+
+def halves(a):
+    high = a.astype(jnp.bfloat16)
+    return high, (a - high.astype(jnp.float32)).astype(jnp.bfloat16)
 
 
 def iota(shape, dim):
@@ -42,13 +54,14 @@
     mrf_ref,
     rrow_ref,
     wrow_ref,
+    rpack_ref,
+    wpack_ref,
     med_ref,
     lng_ref,
     tail_ref,
     coef_ref,
     loc_ref,
     pack_ref,
-    packf_ref,
     slot_ref,
     ysend,
     yrecv,
@@ -66,7 +79,7 @@
     zr_sem,
 ):
     channels, tokens = q_ref.shape
-    order = rates_ref.shape[1]
+    order = rates_ref.shape[0]
     groups = mr_ref.shape[0]
     per = tokens // order
     blocks = groups // per
@@ -90,10 +103,6 @@
         cols = pl.ds(pl.multiple_of(b * e_block, e_block), e_block)
         return pltpu.make_async_copy(w_hbm.at[:, cols], w_ref.at[b], w_sem.at[b])
 
-    @pl.loop(0, n_tp)
-    def _(b):
-        w_copy(b).start()
-
     barrier = pltpu.get_barrier_semaphore()
     for d in range(1, n_ctx):
         pl.semaphore_signal(
@@ -132,29 +141,49 @@
     def _():
         halo_copy.start()
 
+    @pl.loop(0, n_z)
+    def _(p):
+        w_copy(target(p) * 2 + 1 - y).start()
+
+    @pl.loop(0, n_z)
+    def _(p):
+        w_copy(target(p) * 2 + y).start()
+
     @pl.when(i == 0)
     def _():
         halo_ref[...] = jnp.zeros_like(halo_ref)
 
     mrf_ref[...] = mr_ref[...].astype(jnp.float32)
-    rates = rates_ref[...]
-    weights = res_ref[...] * jnp.sqrt(2.0 * rates / order)
+    rates = upright(rates_ref[...], tokens)
+    weights = upright(res_ref[...], tokens) * jnp.sqrt(2.0 * rates / order)
     own = iota((groups, tokens), 1) // order == iota((groups, tokens), 0) % per
-    for src, dst in ((rates, rrow_ref), (weights, wrow_ref)):
+    for src, dst, packed in ((rates, rrow_ref, rpack_ref), (weights, wrow_ref, wpack_ref)):
         wide = jnp.where(own, jnp.concatenate([src] * per, axis=1), 0.0)
         dst[...] = jnp.sum(wide.reshape(blocks, per, tokens), axis=1)
+        parts = [src[k * per : (k + 1) * per] for k in range(blocks)]
+        if blocks < per:
+            parts.append(jnp.zeros((per, (per - blocks) * order), jnp.float32))
+        joined = jnp.concatenate(parts, axis=1)
+        packed[...] = jnp.broadcast_to(
+            joined[:, None, :], (per, chan_group, tokens)
+        ).reshape(span, tokens)
 
     square = (tokens, tokens)
     row_i, col_i = iota(square, 0), iota(square, 1)
     same = row_i // chan_group == col_i // order
 
-    @pl.loop(0, blocks)
+    @pl.loop(0, blocks, unroll=2)
     def _(k):
         r = rrow_ref[pl.ds(k, 1), :]
         place = row_i.astype(jnp.float32)
         exp0 = jnp.exp(-r * place)
-        tail_ref[k] = jnp.exp(-r * (tokens - 1.0 - place))
-        coef_ref[k] = exp0 * jnp.exp(-r)
+        high, low = halves(jnp.exp(-r * (tokens - 1.0 - place)))
+        tail_ref[k, :tokens, :] = high
+        tail_ref[k, tokens:, :] = low
+        high, low = halves(exp0 * jnp.exp(-r))
+        coef_ref[k, :, :tokens] = high
+        coef_ref[k, :, tokens : 2 * tokens] = high
+        coef_ref[k, :, 2 * tokens :] = low
         w_sel = jnp.where(
             iota((per, tokens), 1) // order == iota((per, tokens), 0),
             wrow_ref[pl.ds(k, 1), :],
@@ -177,26 +206,26 @@
                 jnp.bfloat16
             )
 
-    packf_ref[...] = jnp.zeros_like(packf_ref)
-
     @pl.when(i > 0)
     def _():
         halo_copy.wait_recv()
 
-    @pl.loop(0, blocks)
+    @pl.loop(0, blocks, unroll=4 if blocks % 4 == 0 else 1)
     def _(k):
         for g in range(per):
             rows = pl.ds(pl.multiple_of((k * per + g) * chan_group, chan_group), chan_group)
             signal = jnp.concatenate([halo_ref[rows, :], kv_ref[rows, :]], axis=1)
             medium = dot(signal, med_ref[k * per + g])
             gm_ref[rows, :] = (q_ref[rows, :].astype(jnp.float32) * medium).astype(jnp.bfloat16)
-        rows = pl.ds(pl.multiple_of(k * span, span), span)
-        state = dot(gm_ref[rows, :].astype(jnp.float32), tail_ref[k], precision=HIGH)
+
+    packed = jnp.zeros(square, jnp.float32)
+    for k in range(blocks):
+        signal = gm_ref[k * span : (k + 1) * span, :]
+        state = dot(jnp.concatenate([signal, signal], axis=1), tail_ref[k])
         state = jnp.where(same, state, 0.0).astype(jnp.bfloat16)
         spread = jnp.where(col_i == k * order + row_i % order, 1.0, 0.0).astype(jnp.bfloat16)
-        packf_ref[...] += dot(state, spread)
-
-    pack_ref[...] = packf_ref[...].astype(jnp.bfloat16)
+        packed += dot(state, spread)
+    pack_ref[...] = packed.astype(jnp.bfloat16)
 
     def st_copy(d):
         return pltpu.make_async_remote_copy(
@@ -218,7 +247,7 @@
         def _():
             slot_ref[d] = jnp.zeros(square, jnp.bfloat16)
 
-    @pl.loop(0, blocks)
+    @pl.loop(0, blocks, unroll=4 if blocks % 4 == 0 else 1)
     def _(k):
         for g in range(per):
             rows = pl.ds(pl.multiple_of((k * per + g) * chan_group, chan_group), chan_group)
@@ -230,25 +259,23 @@
         def _():
             st_copy(d).wait_recv()
 
-    @pl.loop(0, blocks)
-    def _(k):
-        rows = pl.ds(pl.multiple_of(k * span, span), span)
-        r = rrow_ref[pl.ds(k, 1), :]
-        gather = jnp.where(row_i == k * order + col_i % order, 1.0, 0.0).astype(jnp.bfloat16)
-
-        def add(d, total):
-            fade = jnp.exp(-r * (tokens * d).astype(jnp.float32))
-            return total + fade * dot(slot_ref[d], gather)
-
-        carried = lax.fori_loop(0, n_ctx - 1, add, jnp.zeros(square, jnp.float32))
-        carried = jnp.where(same, carried * wrow_ref[pl.ds(k, 1), :], 0.0)
-        wide = loc_ref[rows, :] + dot(carried, coef_ref[k], ((1,), (1,)), HIGH)
-        gated = og_ref[rows, :].astype(jnp.float32) * wide.astype(jnp.bfloat16).astype(jnp.float32)
+    def add(d, total):
+        fade = jnp.exp(-rpack_ref[...] * (tokens * d).astype(jnp.float32))
+        return total + fade * slot_ref[d].astype(jnp.float32)
+
+    carried = lax.fori_loop(0, n_ctx - 1, add, jnp.zeros(square, jnp.float32))
+    carried = jnp.concatenate(halves(carried * wpack_ref[...]), axis=1)
+    wide_row = iota((2 * tokens, tokens), 0) % tokens
+    wide_col = iota((2 * tokens, tokens), 1)
+    for k in range(blocks):
+        rows = slice(k * span, (k + 1) * span)
+        gather = jnp.where(wide_row == k * order + wide_col % order, 1.0, 0.0)
+        modes = jnp.where(same, dot(carried, gather.astype(jnp.bfloat16)), 0.0)
+        high, low = halves(modes)
+        entered = dot(jnp.concatenate([high, low, high], axis=1), coef_ref[k], ((1,), (1,)))
+        wide = (loc_ref[rows, :] + entered).astype(jnp.bfloat16)
+        gated = og_ref[rows, :].astype(jnp.float32) * wide.astype(jnp.float32)
         gt_ref[:, rows] = gated.T.astype(jnp.bfloat16)
-
-    @pl.loop(0, n_tp)
-    def _(b):
-        w_copy(b).wait()
 
     def y_copy(p, c):
         return pltpu.make_async_remote_copy(
@@ -285,6 +312,7 @@
     @pl.loop(0, n_z)
     def _(p):
         b = target(p) * 2 + 1 - y
+        w_copy(b).wait()
         for c in range(chunks):
             ysend[p, c] = dot(gt_ref[...], w_ref[b, :, c * cw : (c + 1) * cw]).astype(jnp.bfloat16)
             y_copy(p, c).start()
@@ -292,6 +320,7 @@
     @pl.loop(0, n_z)
     def _(p):
         b = target(p) * 2 + y
+        w_copy(b).wait()
         for c in range(chunks):
             acc[p, c] = dot(gt_ref[...], w_ref[b, :, c * cw : (c + 1) * cw])
 
@@ -377,13 +406,14 @@
             pltpu.VMEM((groups, tokens), f32),
             pltpu.VMEM((blocks, tokens), f32),
             pltpu.VMEM((blocks, tokens), f32),
+            pltpu.VMEM((tokens, tokens), f32),
+            pltpu.VMEM((tokens, tokens), f32),
             pltpu.VMEM((groups, 2 * tokens, tokens), bf),
             pltpu.VMEM((groups, tokens, tokens), bf),
-            pltpu.VMEM((blocks, tokens, tokens), f32),
-            pltpu.VMEM((blocks, tokens, tokens), f32),
+            pltpu.VMEM((blocks, 2 * tokens, tokens), bf),
+            pltpu.VMEM((blocks, tokens, 3 * tokens), bf),
             pltpu.VMEM((channels, tokens), f32),
             pltpu.VMEM((tokens, tokens), bf),
-            pltpu.VMEM((tokens, tokens), f32),
             pltpu.VMEM((n_ctx - 1, tokens, tokens), bf),
             pltpu.VMEM((n_z, chunks, tokens, cw), bf),
             pltpu.VMEM((n_z, chunks, tokens, cw), bf),
@@ -404,7 +434,7 @@
             collective_id=0, has_side_effects=True, vmem_limit_bytes=56 * 2**20
         ),
         name="conv_project",
-    )(q, k, v, og, mr, rates, res, w)
+    )(q, k, v, og, mr, rates.T, res.T, w)
 
 
 def solution(mesh):

time: 53.4 us -> 42 us (0.79)
  Pallas kernels: 48.5 us -> 40 us
  local copies, waits for them, and re-layouts: 4.44 us -> 1.67 us
    pallas_call x1, Pallas kernels: 48.5 us -> 40 us  [per_device(): pl.pallas_call(functools.partial(kernel, n_ctx, n_tp), out_shape=jax.Shap...]
    unnamed x3 -> x1, local copies, waits for them, and re-layouts: 4.44 us -> 1.67 us
where the time goes in v2:
time: 42 us; the launch traced here: 41.7 us
  Pallas kernels  40 us (95%)
  local copies, waits for them, and re-layouts  1.67 us (4%)
    pallas_call x1, Pallas kernels, per_device(): pl.pallas_call(functools.partial(kernel, n_ctx, n_tp), out_shape=jax.Shap...  40 us
    unnamed x1, local copies, waits for them, and re-layouts  1.67 us

profile of v2, /device:TPU:26, one launch (start us, length us, event | category | flops | bytes accessed | tf_op | source)
XLA Modules:
  0.0 41.7 jit_solution(13519883722219797177)
XLA Ops:
  0.0 40.0 %conv_project.1 = bf16[1024,128]{1,0:T(8,128)(2,1)} custom-call(bf16[1024,128]{1,0:T(8,128)(2,1)} %q_ref.1, bf16[1024,128]{1,0:T(8,128)(2,1)} %k_ref.1, bf16[1024,128]{1,0:T(8,128)(2,1)} %v_ref.1, bf16[1024,128]{1,0:T(8,128)(2,1)} %og_ref.1, bf16[64,128]{1,0:T(8,128)(2,1)} %mr_ref.1, f32[16,64]{1,0:T(8,128)} %bitcast.2, f32[16,64]{1,0:T(8,128)} %bitcast.3, ...), custom_call_target="tpu_custom_call" | custom-call | tf_op jit(solution)/shard_map/conv_project/pallas_call | solution.py:395
  40.0 1.7 %copy.10 = bf16[1024,128]{1,0:T(8,128)(2,1)} copy(bf16[1024,128]{1,0:T(8,128)(2,1)} %conv_project.1) | data formatting | bytes 524288

commit v3 on v2

--- a/solution.py
+++ b/solution.py
@@ -37,15 +37,19 @@
 def kernel(
     n_ctx,
     n_tp,
-    q_ref,
-    k_ref,
-    v_ref,
-    og_ref,
+    q_hbm,
+    k_hbm,
+    v_hbm,
+    og_hbm,
     mr_ref,
     rates_ref,
     res_ref,
     w_hbm,
     out_ref,
+    q_ref,
+    k_ref,
+    v_ref,
+    og_ref,
     w_ref,
     kv_ref,
     halo_ref,
@@ -68,6 +72,7 @@
     acc,
     zsend,
     zrecv,
+    in_sem,
     w_sem,
     halo_send,
     halo_recv,
@@ -78,7 +83,7 @@
     zs_sem,
     zr_sem,
 ):
-    channels, tokens = q_ref.shape
+    channels, tokens = q_hbm.shape
     order = rates_ref.shape[0]
     groups = mr_ref.shape[0]
     per = tokens // order
@@ -87,6 +92,8 @@
     e_block = out_ref.shape[0]
     cw = ysend.shape[3]
     chunks = e_block // cw
+    half = channels // 2
+    half_blocks = blocks // 2
     n_z = n_tp // 2
     i = lax.axis_index("ctx")
     me = lax.axis_index("tp")
@@ -120,26 +127,41 @@
     def _():
         pl.semaphore_signal(barrier, inc=1, device_id={"tp": me + 2}, device_id_type=MESH)
 
-    kv_ref[...] = (
-        k_ref[...].astype(jnp.float32) * v_ref[...].astype(jnp.float32)
-    ).astype(jnp.bfloat16)
-
-    pl.semaphore_wait(
-        barrier, n_ctx + jnp.where(z > 0, 1, 0) + jnp.where(z < n_z - 1, 1, 0)
-    )
-
-    halo_copy = pltpu.make_async_remote_copy(
-        src_ref=kv_ref,
-        dst_ref=halo_ref,
-        send_sem=halo_send,
-        recv_sem=halo_recv,
-        device_id={"ctx": lax.rem(i + 1, n_ctx)},
-        device_id_type=MESH,
-    )
-
-    @pl.when(i < n_ctx - 1)
-    def _():
-        halo_copy.start()
+    inputs = [
+        pltpu.make_async_copy(src, dst, in_sem.at[n])
+        for n, (src, dst) in enumerate(
+            ((k_hbm, k_ref), (v_hbm, v_ref), (q_hbm, q_ref), (og_hbm, og_ref))
+        )
+    ]
+    for copy in inputs:
+        copy.start()
+
+    def halo_copy(h):
+        rows = pl.ds(h * half, half)
+        return pltpu.make_async_remote_copy(
+            src_ref=kv_ref.at[rows],
+            dst_ref=halo_ref.at[rows],
+            send_sem=halo_send.at[h],
+            recv_sem=halo_recv.at[h],
+            device_id={"ctx": lax.rem(i + 1, n_ctx)},
+            device_id_type=MESH,
+        )
+
+    inputs[0].wait()
+    inputs[1].wait()
+    for h in range(2):
+        rows = slice(h * half, (h + 1) * half)
+        kv_ref[rows] = (
+            k_ref[rows].astype(jnp.float32) * v_ref[rows].astype(jnp.float32)
+        ).astype(jnp.bfloat16)
+        if h == 0:
+            pl.semaphore_wait(
+                barrier, n_ctx + jnp.where(z > 0, 1, 0) + jnp.where(z < n_z - 1, 1, 0)
+            )
+
+        @pl.when(i < n_ctx - 1)
+        def _():
+            halo_copy(h).start()
 
     @pl.loop(0, n_z)
     def _(p):
@@ -206,46 +228,53 @@
                 jnp.bfloat16
             )
 
-    @pl.when(i > 0)
-    def _():
-        halo_copy.wait_recv()
-
-    @pl.loop(0, blocks, unroll=4 if blocks % 4 == 0 else 1)
-    def _(k):
-        for g in range(per):
-            rows = pl.ds(pl.multiple_of((k * per + g) * chan_group, chan_group), chan_group)
-            signal = jnp.concatenate([halo_ref[rows, :], kv_ref[rows, :]], axis=1)
-            medium = dot(signal, med_ref[k * per + g])
-            gm_ref[rows, :] = (q_ref[rows, :].astype(jnp.float32) * medium).astype(jnp.bfloat16)
-
-    packed = jnp.zeros(square, jnp.float32)
-    for k in range(blocks):
-        signal = gm_ref[k * span : (k + 1) * span, :]
-        state = dot(jnp.concatenate([signal, signal], axis=1), tail_ref[k])
-        state = jnp.where(same, state, 0.0).astype(jnp.bfloat16)
-        spread = jnp.where(col_i == k * order + row_i % order, 1.0, 0.0).astype(jnp.bfloat16)
-        packed += dot(state, spread)
-    pack_ref[...] = packed.astype(jnp.bfloat16)
-
-    def st_copy(d):
+    def st_copy(d, h):
         return pltpu.make_async_remote_copy(
-            src_ref=pack_ref,
-            dst_ref=slot_ref.at[d],
-            send_sem=st_send.at[d],
-            recv_sem=st_recv.at[d],
+            src_ref=pack_ref.at[h],
+            dst_ref=slot_ref.at[d, h],
+            send_sem=st_send.at[d, h],
+            recv_sem=st_recv.at[d, h],
             device_id={"ctx": lax.rem(i + d + 1, n_ctx)},
             device_id_type=MESH,
         )
 
     @pl.loop(0, n_ctx - 1)
     def _(d):
-        @pl.when(i + d + 1 < n_ctx)
-        def _():
-            st_copy(d).start()
-
         @pl.when(i < d + 1)
         def _():
-            slot_ref[d] = jnp.zeros(square, jnp.bfloat16)
+            slot_ref[d] = jnp.zeros((2,) + square, jnp.bfloat16)
+
+    inputs[2].wait()
+    for h in range(2):
+
+        @pl.when(i > 0)
+        def _():
+            halo_copy(h).wait_recv()
+
+        @pl.loop(h * half_blocks, (h + 1) * half_blocks, unroll=half_blocks)
+        def _(k):
+            for g in range(per):
+                rows = pl.ds(pl.multiple_of((k * per + g) * chan_group, chan_group), chan_group)
+                signal = jnp.concatenate([halo_ref[rows, :], kv_ref[rows, :]], axis=1)
+                medium = dot(signal, med_ref[k * per + g])
+                gm_ref[rows, :] = (q_ref[rows, :].astype(jnp.float32) * medium).astype(
+                    jnp.bfloat16
+                )
+
+        packed = jnp.zeros(square, jnp.float32)
+        for k in range(h * half_blocks, (h + 1) * half_blocks):
+            signal = gm_ref[k * span : (k + 1) * span, :]
+            state = dot(jnp.concatenate([signal, signal], axis=1), tail_ref[k])
+            state = jnp.where(same, state, 0.0).astype(jnp.bfloat16)
+            spread = jnp.where(col_i == k * order + row_i % order, 1.0, 0.0)
+            packed += dot(state, spread.astype(jnp.bfloat16))
+        pack_ref[h] = packed.astype(jnp.bfloat16)
+
+        @pl.loop(0, n_ctx - 1)
+        def _(d):
+            @pl.when(i + d + 1 < n_ctx)
+            def _():
+                st_copy(d, h).start()
 
     @pl.loop(0, blocks, unroll=4 if blocks % 4 == 0 else 1)
     def _(k):
@@ -253,29 +282,32 @@
             rows = pl.ds(pl.multiple_of((k * per + g) * chan_group, chan_group), chan_group)
             loc_ref[rows, :] = dot(gm_ref[rows, :], lng_ref[k * per + g])
 
-    @pl.loop(0, n_ctx - 1)
-    def _(d):
-        @pl.when(i >= d + 1)
-        def _():
-            st_copy(d).wait_recv()
-
-    def add(d, total):
-        fade = jnp.exp(-rpack_ref[...] * (tokens * d).astype(jnp.float32))
-        return total + fade * slot_ref[d].astype(jnp.float32)
-
-    carried = lax.fori_loop(0, n_ctx - 1, add, jnp.zeros(square, jnp.float32))
-    carried = jnp.concatenate(halves(carried * wpack_ref[...]), axis=1)
+    inputs[3].wait()
     wide_row = iota((2 * tokens, tokens), 0) % tokens
     wide_col = iota((2 * tokens, tokens), 1)
-    for k in range(blocks):
-        rows = slice(k * span, (k + 1) * span)
-        gather = jnp.where(wide_row == k * order + wide_col % order, 1.0, 0.0)
-        modes = jnp.where(same, dot(carried, gather.astype(jnp.bfloat16)), 0.0)
-        high, low = halves(modes)
-        entered = dot(jnp.concatenate([high, low, high], axis=1), coef_ref[k], ((1,), (1,)))
-        wide = (loc_ref[rows, :] + entered).astype(jnp.bfloat16)
-        gated = og_ref[rows, :].astype(jnp.float32) * wide.astype(jnp.float32)
-        gt_ref[:, rows] = gated.T.astype(jnp.bfloat16)
+    for h in range(2):
+
+        @pl.loop(0, n_ctx - 1)
+        def _(d):
+            @pl.when(i >= d + 1)
+            def _():
+                st_copy(d, h).wait_recv()
+
+        def add(d, total):
+            fade = jnp.exp(-rpack_ref[...] * (tokens * d).astype(jnp.float32))
+            return total + fade * slot_ref[d, h].astype(jnp.float32)
+
+        carried = lax.fori_loop(0, n_ctx - 1, add, jnp.zeros(square, jnp.float32))
+        carried = jnp.concatenate(halves(carried * wpack_ref[...]), axis=1)
+        for k in range(h * half_blocks, (h + 1) * half_blocks):
+            rows = slice(k * span, (k + 1) * span)
+            gather = jnp.where(wide_row == k * order + wide_col % order, 1.0, 0.0)
+            modes = jnp.where(same, dot(carried, gather.astype(jnp.bfloat16)), 0.0)
+            high, low = halves(modes)
+            entered = dot(jnp.concatenate([high, low, high], axis=1), coef_ref[k], ((1,), (1,)))
+            wide = (loc_ref[rows, :] + entered).astype(jnp.bfloat16)
+            gated = og_ref[rows, :].astype(jnp.float32) * wide.astype(jnp.float32)
+            gt_ref[:, rows] = gated.T.astype(jnp.bfloat16)
 
     def y_copy(p, c):
         return pltpu.make_async_remote_copy(
@@ -361,13 +393,15 @@
 
     @pl.when(i < n_ctx - 1)
     def _():
-        halo_copy.wait_send()
+        for h in range(2):
+            halo_copy(h).wait_send()
 
     @pl.loop(0, n_ctx - 1)
     def _(d):
         @pl.when(i + d + 1 < n_ctx)
         def _():
-            st_copy(d).wait_send()
+            for h in range(2):
+                st_copy(d, h).wait_send()
 
     @pl.loop(0, n_z)
     def _(p):
@@ -383,7 +417,7 @@
 def per_device(n_ctx, n_tp, q, k, v, og, mr, rates, res, w):
     channels, tokens = q.shape
     groups, order = rates.shape
-    assert tokens == mr.shape[1] and tokens % order == 0 and n_tp % 2 == 0
+    assert tokens == mr.shape[1] and groups * order % (2 * tokens) == 0 and tokens % order == 0 and n_tp % 2 == 0
     blocks = groups * order // tokens
     e_block = w.shape[1] // n_tp
     cw = min(e_block, 256)
@@ -391,13 +425,18 @@
     n_z = n_tp // 2
     bf, f32 = jnp.bfloat16, jnp.float32
     dma = pltpu.SemaphoreType.DMA
+    anywhere = pl.BlockSpec(memory_space=pl.ANY)
     vmem = pl.BlockSpec(memory_space=pltpu.VMEM)
     return pl.pallas_call(
         functools.partial(kernel, n_ctx, n_tp),
         out_shape=jax.ShapeDtypeStruct((e_block, tokens), bf),
-        in_specs=[vmem] * 7 + [pl.BlockSpec(memory_space=pl.ANY)],
+        in_specs=[anywhere] * 4 + [vmem] * 3 + [anywhere],
         out_specs=vmem,
         scratch_shapes=[
+            pltpu.VMEM((channels, tokens), bf),
+            pltpu.VMEM((channels, tokens), bf),
+            pltpu.VMEM((channels, tokens), bf),
+            pltpu.VMEM((channels, tokens), bf),
             pltpu.VMEM((n_tp, channels, e_block), bf),
             pltpu.VMEM((channels, tokens), bf),
             pltpu.VMEM((channels, tokens), bf),
@@ -413,18 +452,19 @@
             pltpu.VMEM((blocks, 2 * tokens, tokens), bf),
             pltpu.VMEM((blocks, tokens, 3 * tokens), bf),
             pltpu.VMEM((channels, tokens), f32),
-            pltpu.VMEM((tokens, tokens), bf),
-            pltpu.VMEM((n_ctx - 1, tokens, tokens), bf),
+            pltpu.VMEM((2, tokens, tokens), bf),
+            pltpu.VMEM((n_ctx - 1, 2, tokens, tokens), bf),
             pltpu.VMEM((n_z, chunks, tokens, cw), bf),
             pltpu.VMEM((n_z, chunks, tokens, cw), bf),
             pltpu.VMEM((n_z, chunks, tokens, cw), f32),
             pltpu.VMEM((n_z, chunks, tokens, cw), bf),
             pltpu.VMEM((2, n_z, chunks, tokens, cw), bf),
+            dma((4,)),
             dma((n_tp,)),
-            dma,
-            dma,
-            dma((n_ctx - 1,)),
-            dma((n_ctx - 1,)),
+            dma((2,)),
+            dma((2,)),
+            dma((n_ctx - 1, 2)),
+            dma((n_ctx - 1, 2)),
             dma((n_z, chunks)),
             dma((n_z, chunks)),
             dma((n_z, chunks)),

time: 42 us -> 42.1 us (level)
  no operation moved by 1% of the time
where the time goes in v3:
time: 42.1 us; the launch traced here: 41.7 us
  Pallas kernels  40 us (95%)
  local copies, waits for them, and re-layouts  1.67 us (4%)
    pallas_call x1, Pallas kernels, per_device(): pl.pallas_call(functools.partial(kernel, n_ctx, n_tp), out_shape=jax.Shap...  40 us
    unnamed x1, local copies, waits for them, and re-layouts  1.67 us

profile of v3, /device:TPU:26, one launch (start us, length us, event | category | flops | bytes accessed | tf_op | source)
XLA Modules:
  0.0 41.7 jit_solution(5487893478547957235)
XLA Ops:
  0.0 40.0 %conv_project.1 = bf16[1024,128]{1,0:T(8,128)(2,1)} custom-call(bf16[1024,128]{1,0:T(8,128)(2,1)} %q_hbm.1, bf16[1024,128]{1,0:T(8,128)(2,1)} %k_hbm.1, bf16[1024,128]{1,0:T(8,128)(2,1)} %v_hbm.1, bf16[1024,128]{1,0:T(8,128)(2,1)} %og_hbm.1, bf16[64,128]{1,0:T(8,128)(2,1)} %mr_ref.1, f32[16,64]{1,0:T(8,128)} %bitcast.2, f32[16,64]{1,0:T(8,128)} %bitcast.3, ...), custom_call_target="tpu_custom_call" | custom-call | tf_op jit(solution)/shard_map/conv_project/pallas_call | solution.py:430
  40.0 1.7 %copy.10 = bf16[1024,128]{1,0:T(8,128)(2,1)} copy(bf16[1024,128]{1,0:T(8,128)(2,1)} %conv_project.1) | data formatting | bytes 524288

commit v4 on v3

--- a/solution.py
+++ b/solution.py
@@ -72,6 +72,9 @@
     acc,
     zsend,
     zrecv,
+    xsend,
+    xrecv,
+    xacc,
     in_sem,
     w_sem,
     halo_send,
@@ -82,6 +85,8 @@
     yr_sem,
     zs_sem,
     zr_sem,
+    xs_sem,
+    xr_sem,
 ):
     channels, tokens = q_hbm.shape
     order = rates_ref.shape[0]
@@ -92,6 +97,7 @@
     e_block = out_ref.shape[0]
     cw = ysend.shape[3]
     chunks = e_block // cw
+    first = chunks // 2
     half = channels // 2
     half_blocks = blocks // 2
     n_z = n_tp // 2
@@ -101,10 +107,11 @@
     y = me % 2
 
     def target(p):
-        q = n_z - 1 - p
-        low = q - jnp.where(q <= z, 1, 0)
-        high = p + jnp.where(p >= z, 1, 0)
-        return jnp.where(p == n_z - 1, z, jnp.where(z < n_z // 2, low, high))
+        t = jnp.where(z < n_z // 2, z, n_z - 1 - z)
+        j = p + jnp.where(p >= jnp.where(t == 0, 1, n_z - t), 1, 0)
+        s = jnp.where(j == 0, n_z - 1, jnp.where(j == 1, 0, n_z - j))
+        s = jnp.where(p == n_z - 1, t, s)
+        return jnp.where(z < n_z // 2, s, n_z - 1 - s)
 
     def w_copy(b):
         cols = pl.ds(pl.multiple_of(b * e_block, e_block), e_block)
@@ -341,41 +348,116 @@
             device_id_type=MESH,
         ).wait_recv()
 
+    def x_copy(p, c):
+        zt = target(p)
+        back = jnp.where(zt < z, 1, 0)
+        end = jnp.where(zt == 0, 0, 1)
+        return pltpu.make_async_remote_copy(
+            src_ref=xsend.at[end, c],
+            dst_ref=xrecv.at[end, c],
+            send_sem=xs_sem.at[end, c],
+            recv_sem=xr_sem.at[end, c],
+            device_id={"tp": lax.rem(me + 2 - 4 * back + n_tp, n_tp)},
+            device_id_type=MESH,
+        )
+
+    def x_wait(end, c):
+        pltpu.make_async_remote_copy(
+            src_ref=xsend.at[end, c],
+            dst_ref=xrecv.at[end, c],
+            send_sem=xs_sem.at[end, c],
+            recv_sem=xr_sem.at[end, c],
+            device_id={"tp": z * 2 + 1 - y},
+            device_id_type=MESH,
+        ).wait_recv()
+
+    def at_end(zt):
+        return jnp.logical_or(zt == 0, zt == n_z - 1)
+
+    def send_own(p, c):
+        zsend[p, c] = acc[p, c].astype(jnp.bfloat16)
+        z_copy(p, c).start()
+
+    def send_other(p, c):
+        end = jnp.where(target(p) == 0, 0, 1)
+        xsend[end, c] = xacc[end, c].astype(jnp.bfloat16)
+        x_copy(p, c).start()
+
     @pl.loop(0, n_z)
     def _(p):
-        b = target(p) * 2 + 1 - y
-        w_copy(b).wait()
+        zt = target(p)
+        end = jnp.where(zt == 0, 0, 1)
+        joins = jnp.where(zt < z, z < n_z - 1, z > 0)
+        w_copy(zt * 2 + 1 - y).wait()
+        w_copy(zt * 2 + y).wait()
         for c in range(chunks):
-            ysend[p, c] = dot(gt_ref[...], w_ref[b, :, c * cw : (c + 1) * cw]).astype(jnp.bfloat16)
-            y_copy(p, c).start()
-
-    @pl.loop(0, n_z)
-    def _(p):
-        b = target(p) * 2 + y
-        w_copy(b).wait()
-        for c in range(chunks):
-            acc[p, c] = dot(gt_ref[...], w_ref[b, :, c * cw : (c + 1) * cw])
+            cols = slice(c * cw, (c + 1) * cw)
+            other = dot(gt_ref[...], w_ref[zt * 2 + 1 - y, :, cols])
+
+            def across():
+                ysend[p, c] = other.astype(jnp.bfloat16)
+                y_copy(p, c).start()
+
+            if c < first:
+
+                @pl.when(at_end(zt))
+                def _():
+                    xacc[end, c] = other
+
+                pl.when(jnp.logical_not(at_end(zt)))(across)
+            else:
+                across()
+            acc[p, c] = dot(gt_ref[...], w_ref[zt * 2 + y, :, cols])
+            if c < first:
+
+                @pl.when(at_end(zt) & (zt != z) & jnp.logical_not(joins))
+                def _():
+                    send_own(p, c)
+                    send_other(p, c)
 
     @pl.loop(0, n_z - 1)
     def _(p):
         zt = target(p)
+        end = jnp.where(zt == 0, 0, 1)
         back = jnp.where(zt < z, 1, 0)
         joins = jnp.where(zt < z, z < n_z - 1, z > 0)
 
         @pl.loop(0, chunks)
         def _(c):
-            y_copy(p, c).wait_recv()
-            acc[p, c] += yrecv[p, c].astype(jnp.float32)
+            ahead = at_end(zt) & (c < first)
+
+            @pl.when(jnp.logical_not(ahead))
+            def _():
+                y_copy(p, c).wait_recv()
+                acc[p, c] += yrecv[p, c].astype(jnp.float32)
 
             @pl.when(joins)
             def _():
                 z_wait(back, zt, c)
                 acc[p, c] += zrecv[back, zt, c].astype(jnp.float32)
 
-            zsend[p, c] = acc[p, c].astype(jnp.bfloat16)
-            z_copy(p, c).start()
-
-    for c in range(chunks):
+            @pl.when(jnp.logical_not(ahead & jnp.logical_not(joins)))
+            def _():
+                send_own(p, c)
+
+            @pl.when(ahead & joins)
+            def _():
+                x_wait(end, c)
+                xacc[end, c] += xrecv[end, c].astype(jnp.float32)
+                send_other(p, c)
+
+    own_end = jnp.where(z == 0, 0, 1)
+
+    @pl.when(at_end(z))
+    def _():
+        for c in range(first):
+            x_wait(own_end, c)
+            ysend[n_z - 1, c] = (
+                xacc[own_end, c] + xrecv[own_end, c].astype(jnp.float32)
+            ).astype(jnp.bfloat16)
+            y_copy(n_z - 1, c).start()
+
+    for c in list(range(first, chunks)) + list(range(first)):
         y_copy(n_z - 1, c).wait_recv()
         acc[n_z - 1, c] += yrecv[n_z - 1, c].astype(jnp.float32)
 
@@ -406,7 +488,18 @@
     @pl.loop(0, n_z)
     def _(p):
         for c in range(chunks):
-            y_copy(p, c).wait_send()
+            if c < first:
+
+                @pl.when(jnp.logical_not(at_end(target(p)) & (p < n_z - 1)))
+                def _():
+                    y_copy(p, c).wait_send()
+
+                @pl.when(at_end(target(p)) & (p < n_z - 1))
+                def _():
+                    x_copy(p, c).wait_send()
+
+            else:
+                y_copy(p, c).wait_send()
 
     @pl.loop(0, n_z - 1)
     def _(p):
@@ -422,6 +515,7 @@
     e_block = w.shape[1] // n_tp
     cw = min(e_block, 256)
     chunks = e_block // cw
+    some = max(1, chunks // 2)
     n_z = n_tp // 2
     bf, f32 = jnp.bfloat16, jnp.float32
     dma = pltpu.SemaphoreType.DMA
@@ -459,6 +553,9 @@
             pltpu.VMEM((n_z, chunks, tokens, cw), f32),
             pltpu.VMEM((n_z, chunks, tokens, cw), bf),
             pltpu.VMEM((2, n_z, chunks, tokens, cw), bf),
+            pltpu.VMEM((2, some, tokens, cw), bf),
+            pltpu.VMEM((2, some, tokens, cw), bf),
+            pltpu.VMEM((2, some, tokens, cw), f32),
             dma((4,)),
             dma((n_tp,)),
             dma((2,)),
@@ -469,6 +566,8 @@
             dma((n_z, chunks)),
             dma((n_z, chunks)),
             dma((2, n_z, chunks)),
+            dma((2, some)),
+            dma((2, some)),
         ],
         compiler_params=pltpu.CompilerParams(
             collective_id=0, has_side_effects=True, vmem_limit_bytes=56 * 2**20

time: 42.1 us -> 41.6 us (0.988)
  the two profiles are of different devices: /device:TPU:26 before, /device:TPU:18 now
where the time goes in v4:
time: 41.6 us; the launch traced here: 41.3 us
  Pallas kernels  39.6 us (95%)
  local copies, waits for them, and re-layouts  1.67 us (4%)
    pallas_call x1, Pallas kernels, per_device(): pl.pallas_call(functools.partial(kernel, n_ctx, n_tp), out_shape=jax.Shap...  39.6 us
    unnamed x1, local copies, waits for them, and re-layouts  1.67 us

profile of v4, /device:TPU:18, one launch (start us, length us, event | category | flops | bytes accessed | tf_op | source)
XLA Modules:
  0.0 41.3 jit_solution(10481414916963326083)
XLA Ops:
  0.0 39.6 %conv_project.1 = bf16[1024,128]{1,0:T(8,128)(2,1)} custom-call(bf16[1024,128]{1,0:T(8,128)(2,1)} %q_hbm.1, bf16[1024,128]{1,0:T(8,128)(2,1)} %k_hbm.1, bf16[1024,128]{1,0:T(8,128)(2,1)} %v_hbm.1, bf16[1024,128]{1,0:T(8,128)(2,1)} %og_hbm.1, bf16[64,128]{1,0:T(8,128)(2,1)} %mr_ref.1, f32[16,64]{1,0:T(8,128)} %bitcast.2, f32[16,64]{1,0:T(8,128)} %bitcast.3, ...), custom_call_target="tpu_custom_call" | custom-call | tf_op jit(solution)/shard_map/conv_project/pallas_call | solution.py:524
  39.7 1.7 %copy.10 = bf16[1024,128]{1,0:T(8,128)(2,1)} copy(bf16[1024,128]{1,0:T(8,128)(2,1)} %conv_project.1) | data formatting | bytes 524288

commit v5 on v4

--- a/solution.py
+++ b/solution.py
@@ -9,13 +9,10 @@
 
 chan_group = 16
 MESH = pl.DeviceIdType.MESH
-HIGH = lax.Precision.HIGHEST
-
-
-def dot(a, b, dims=((1,), (0,)), precision=None):
-    return lax.dot_general(
-        a, b, (dims, ((), ())), preferred_element_type=jnp.float32, precision=precision
-    )
+
+
+def dot(a, b, dims=((1,), (0,))):
+    return lax.dot_general(a, b, (dims, ((), ())), preferred_element_type=jnp.float32)
 
 
 def upright(a, size):
@@ -61,7 +58,7 @@
     rpack_ref,
     wpack_ref,
     med_ref,
-    lng_ref,
+    taps_ref,
     tail_ref,
     coef_ref,
     loc_ref,
@@ -97,7 +94,7 @@
     e_block = out_ref.shape[0]
     cw = ysend.shape[3]
     chunks = e_block // cw
-    first = chunks // 2
+    first = chunks // 4
     half = channels // 2
     half_blocks = blocks // 2
     n_z = n_tp // 2
@@ -199,35 +196,33 @@
 
     square = (tokens, tokens)
     row_i, col_i = iota(square, 0), iota(square, 1)
+    def around(row):
+        return pltpu.roll(jnp.broadcast_to(row, square), 0, 1, stride=1, stride_axis=0)
+
     same = row_i // chan_group == col_i // order
 
-    @pl.loop(0, blocks, unroll=2)
+    @pl.loop(0, blocks, unroll=half_blocks)
     def _(k):
         r = rrow_ref[pl.ds(k, 1), :]
         place = row_i.astype(jnp.float32)
-        exp0 = jnp.exp(-r * place)
         high, low = halves(jnp.exp(-r * (tokens - 1.0 - place)))
         tail_ref[k, :tokens, :] = high
         tail_ref[k, tokens:, :] = low
-        high, low = halves(exp0 * jnp.exp(-r))
-        coef_ref[k, :, :tokens] = high
-        coef_ref[k, :, tokens : 2 * tokens] = high
-        coef_ref[k, :, 2 * tokens :] = low
+        high, low = halves(jnp.exp(-r * place))
+        coef = jnp.concatenate([high, high, low], axis=1)
+        coef_ref[k] = coef
         w_sel = jnp.where(
             iota((per, tokens), 1) // order == iota((per, tokens), 0),
             wrow_ref[pl.ds(k, 1), :],
             0.0,
         )
-        taps = dot(w_sel, exp0, ((1,), (1,)), HIGH)
-        mr = mrf_ref[pl.ds(pl.multiple_of(k * per, per), per), :]
+        w_high, w_low = halves(w_sel)
+        group_rows = pl.ds(pl.multiple_of(k * per, per), per)
+        w_parts = jnp.concatenate([w_high, w_low, w_high], axis=1)
+        taps_ref[group_rows, :] = dot(w_parts, coef, ((1,), (1,)))
+        mr = mrf_ref[group_rows, :]
         for g in range(per):
-            circ = pltpu.roll(
-                jnp.broadcast_to(taps[g : g + 1, :], square), 0, 1, stride=1, stride_axis=0
-            )
-            lng_ref[k * per + g] = jnp.where(row_i <= col_i, circ, 0.0).astype(jnp.bfloat16)
-            circ = pltpu.roll(
-                jnp.broadcast_to(mr[g : g + 1, :], square), 0, 1, stride=1, stride_axis=0
-            )
+            circ = around(mr[g : g + 1, :])
             med_ref[k * per + g, :tokens, :] = jnp.where(row_i > col_i, circ, 0.0).astype(
                 jnp.bfloat16
             )
@@ -283,11 +278,13 @@
             def _():
                 st_copy(d, h).start()
 
-    @pl.loop(0, blocks, unroll=4 if blocks % 4 == 0 else 1)
+    @pl.loop(0, blocks, unroll=half_blocks)
     def _(k):
+        taps = taps_ref[pl.ds(pl.multiple_of(k * per, per), per), :]
         for g in range(per):
             rows = pl.ds(pl.multiple_of((k * per + g) * chan_group, chan_group), chan_group)
-            loc_ref[rows, :] = dot(gm_ref[rows, :], lng_ref[k * per + g])
+            circ = jnp.where(row_i <= col_i, around(taps[g : g + 1, :]), 0.0)
+            loc_ref[rows, :] = dot(gm_ref[rows, :], circ.astype(jnp.bfloat16))
 
     inputs[3].wait()
     wide_row = iota((2 * tokens, tokens), 0) % tokens
@@ -301,7 +298,7 @@
                 st_copy(d, h).wait_recv()
 
         def add(d, total):
-            fade = jnp.exp(-rpack_ref[...] * (tokens * d).astype(jnp.float32))
+            fade = jnp.exp(-rpack_ref[...] * (tokens * d + 1).astype(jnp.float32))
             return total + fade * slot_ref[d, h].astype(jnp.float32)
 
         carried = lax.fori_loop(0, n_ctx - 1, add, jnp.zeros(square, jnp.float32))
@@ -515,7 +512,7 @@
     e_block = w.shape[1] // n_tp
     cw = min(e_block, 256)
     chunks = e_block // cw
-    some = max(1, chunks // 2)
+    some = max(1, chunks // 4)
     n_z = n_tp // 2
     bf, f32 = jnp.bfloat16, jnp.float32
     dma = pltpu.SemaphoreType.DMA
@@ -542,7 +539,7 @@
             pltpu.VMEM((tokens, tokens), f32),
             pltpu.VMEM((tokens, tokens), f32),
             pltpu.VMEM((groups, 2 * tokens, tokens), bf),
-            pltpu.VMEM((groups, tokens, tokens), bf),
+            pltpu.VMEM((groups, tokens), f32),
             pltpu.VMEM((blocks, 2 * tokens, tokens), bf),
             pltpu.VMEM((blocks, tokens, 3 * tokens), bf),
             pltpu.VMEM((channels, tokens), f32),

time: 41.6 us -> 39.3 us (0.945)
  the two profiles are of different devices: /device:TPU:18 before, /device:TPU:22 now
where the time goes in v5:
time: 39.3 us; the launch traced here: 39.1 us
  Pallas kernels  37.4 us (95%)
  local copies, waits for them, and re-layouts  1.67 us (4%)
    pallas_call x1, Pallas kernels, per_device(): pl.pallas_call(functools.partial(kernel, n_ctx, n_tp), out_shape=jax.Shap...  37.4 us
    unnamed x1, local copies, waits for them, and re-layouts  1.67 us

profile of v5, /device:TPU:22, one launch (start us, length us, event | category | flops | bytes accessed | tf_op | source)
XLA Modules:
  0.0 39.1 jit_solution(1217537868725631419)
XLA Ops:
  0.0 37.4 %conv_project.1 = bf16[1024,128]{1,0:T(8,128)(2,1)} custom-call(bf16[1024,128]{1,0:T(8,128)(2,1)} %q_hbm.1, bf16[1024,128]{1,0:T(8,128)(2,1)} %k_hbm.1, bf16[1024,128]{1,0:T(8,128)(2,1)} %v_hbm.1, bf16[1024,128]{1,0:T(8,128)(2,1)} %og_hbm.1, bf16[64,128]{1,0:T(8,128)(2,1)} %mr_ref.1, f32[16,64]{1,0:T(8,128)} %bitcast.2, f32[16,64]{1,0:T(8,128)} %bitcast.3, ...), custom_call_target="tpu_custom_call" | custom-call | tf_op jit(solution)/shard_map/conv_project/pallas_call | solution.py:521
  37.4 1.7 %copy.10 = bf16[1024,128]{1,0:T(8,128)(2,1)} copy(bf16[1024,128]{1,0:T(8,128)(2,1)} %conv_project.1) | data formatting | bytes 524288

commit v6 on v5

--- a/solution.py
+++ b/solution.py
@@ -167,14 +167,6 @@
         def _():
             halo_copy(h).start()
 
-    @pl.loop(0, n_z)
-    def _(p):
-        w_copy(target(p) * 2 + 1 - y).start()
-
-    @pl.loop(0, n_z)
-    def _(p):
-        w_copy(target(p) * 2 + y).start()
-
     @pl.when(i == 0)
     def _():
         halo_ref[...] = jnp.zeros_like(halo_ref)
@@ -246,6 +238,17 @@
         def _():
             slot_ref[d] = jnp.zeros((2,) + square, jnp.bfloat16)
 
+    @pl.loop(0, blocks, unroll=half_blocks)
+    def _(k):
+        for g in range(per):
+            rows = pl.ds(pl.multiple_of((k * per + g) * chan_group, chan_group), chan_group)
+            loc_ref[rows, :] = dot(kv_ref[rows, :], med_ref[k * per + g, tokens:, :])
+
+    @pl.loop(0, n_z)
+    def _(p):
+        w_copy(target(p) * 2 + 1 - y).start()
+        w_copy(target(p) * 2 + y).start()
+
     inputs[2].wait()
     for h in range(2):
 
@@ -257,8 +260,7 @@
         def _(k):
             for g in range(per):
                 rows = pl.ds(pl.multiple_of((k * per + g) * chan_group, chan_group), chan_group)
-                signal = jnp.concatenate([halo_ref[rows, :], kv_ref[rows, :]], axis=1)
-                medium = dot(signal, med_ref[k * per + g])
+                medium = loc_ref[rows, :] + dot(halo_ref[rows, :], med_ref[k * per + g, :tokens, :])
                 gm_ref[rows, :] = (q_ref[rows, :].astype(jnp.float32) * medium).astype(
                     jnp.bfloat16
                 )

time: 39.3 us -> 39.4 us (level)
  the two profiles are of different devices: /device:TPU:22 before, /device:TPU:18 now
where the time goes in v6:
time: 39.4 us; the launch traced here: 39.2 us
  Pallas kernels  37.5 us (95%)
  local copies, waits for them, and re-layouts  1.67 us (4%)
    pallas_call x1, Pallas kernels, per_device(): pl.pallas_call(functools.partial(kernel, n_ctx, n_tp), out_shape=jax.Shap...  37.5 us
    unnamed x1, local copies, waits for them, and re-layouts  1.67 us

profile of v6, /device:TPU:18, one launch (start us, length us, event | category | flops | bytes accessed | tf_op | source)
XLA Modules:
  0.0 39.2 jit_solution(11476271417742689256)
XLA Ops:
  0.0 37.5 %conv_project.1 = bf16[1024,128]{1,0:T(8,128)(2,1)} custom-call(bf16[1024,128]{1,0:T(8,128)(2,1)} %q_hbm.1, bf16[1024,128]{1,0:T(8,128)(2,1)} %k_hbm.1, bf16[1024,128]{1,0:T(8,128)(2,1)} %v_hbm.1, bf16[1024,128]{1,0:T(8,128)(2,1)} %og_hbm.1, bf16[64,128]{1,0:T(8,128)(2,1)} %mr_ref.1, f32[16,64]{1,0:T(8,128)} %bitcast.2, f32[16,64]{1,0:T(8,128)} %bitcast.3, ...), custom_call_target="tpu_custom_call" | custom-call | tf_op jit(solution)/shard_map/conv_project/pallas_call | solution.py:523
  37.5 1.7 %copy.10 = bf16[1024,128]{1,0:T(8,128)(2,1)} copy(bf16[1024,128]{1,0:T(8,128)(2,1)} %conv_project.1) | data formatting | bytes 524288

commit v7 on v5

--- a/solution.py
+++ b/solution.py
@@ -94,6 +94,7 @@
     e_block = out_ref.shape[0]
     cw = ysend.shape[3]
     chunks = e_block // cw
+    pair = 2 if chunks % 2 == 0 else 1
     first = chunks // 4
     half = channels // 2
     half_blocks = blocks // 2
@@ -388,8 +389,12 @@
         w_copy(zt * 2 + 1 - y).wait()
         w_copy(zt * 2 + y).wait()
         for c in range(chunks):
-            cols = slice(c * cw, (c + 1) * cw)
-            other = dot(gt_ref[...], w_ref[zt * 2 + 1 - y, :, cols])
+            if c % pair == 0:
+                cols = slice(c * cw, (c + pair) * cw)
+                both = dot(gt_ref[...], w_ref[zt * 2 + 1 - y, :, cols])
+                mine = dot(gt_ref[...], w_ref[zt * 2 + y, :, cols])
+            part = slice(c % pair * cw, (c % pair + 1) * cw)
+            other = both[:, part]
 
             def across():
                 ysend[p, c] = other.astype(jnp.bfloat16)
@@ -404,7 +409,7 @@
                 pl.when(jnp.logical_not(at_end(zt)))(across)
             else:
                 across()
-            acc[p, c] = dot(gt_ref[...], w_ref[zt * 2 + y, :, cols])
+            acc[p, c] = mine[:, part]
             if c < first:
 
                 @pl.when(at_end(zt) & (zt != z) & jnp.logical_not(joins))
@@ -510,7 +515,7 @@
     assert tokens == mr.shape[1] and groups * order % (2 * tokens) == 0 and tokens % order == 0 and n_tp % 2 == 0
     blocks = groups * order // tokens
     e_block = w.shape[1] // n_tp
-    cw = min(e_block, 256)
+    cw = min(e_block, 128)
     chunks = e_block // cw
     some = max(1, chunks // 4)
     n_z = n_tp // 2

time: 39.3 us -> 38.9 us (0.990)
  the two profiles are of different devices: /device:TPU:22 before, /device:TPU:26 now
where the time goes in v7:
time: 38.9 us; the launch traced here: 38.7 us
  Pallas kernels  37 us (95%)
  local copies, waits for them, and re-layouts  1.67 us (4%)
    pallas_call x1, Pallas kernels, per_device(): pl.pallas_call(functools.partial(kernel, n_ctx, n_tp), out_shape=jax.Shap...  37 us
    unnamed x1, local copies, waits for them, and re-layouts  1.67 us

profile of v7, /device:TPU:26, one launch (start us, length us, event | category | flops | bytes accessed | tf_op | source)
XLA Modules:
  0.0 38.7 jit_solution(3279064124473497270)
XLA Ops:
  0.0 37.0 %conv_project.1 = bf16[1024,128]{1,0:T(8,128)(2,1)} custom-call(bf16[1024,128]{1,0:T(8,128)(2,1)} %q_hbm.1, bf16[1024,128]{1,0:T(8,128)(2,1)} %k_hbm.1, bf16[1024,128]{1,0:T(8,128)(2,1)} %v_hbm.1, bf16[1024,128]{1,0:T(8,128)(2,1)} %og_hbm.1, bf16[64,128]{1,0:T(8,128)(2,1)} %mr_ref.1, f32[16,64]{1,0:T(8,128)} %bitcast.2, f32[16,64]{1,0:T(8,128)} %bitcast.3, ...), custom_call_target="tpu_custom_call" | custom-call | tf_op jit(solution)/shard_map/conv_project/pallas_call | solution.py:526
  37.0 1.7 %copy.10 = bf16[1024,128]{1,0:T(8,128)(2,1)} copy(bf16[1024,128]{1,0:T(8,128)(2,1)} %conv_project.1) | data formatting | bytes 524288

commit v8 on v7

--- a/solution.py
+++ b/solution.py
@@ -95,7 +95,7 @@
     cw = ysend.shape[3]
     chunks = e_block // cw
     pair = 2 if chunks % 2 == 0 else 1
-    first = chunks // 4
+    first = 3 * chunks // 8
     half = channels // 2
     half_blocks = blocks // 2
     n_z = n_tp // 2
@@ -517,7 +517,7 @@
     e_block = w.shape[1] // n_tp
     cw = min(e_block, 128)
     chunks = e_block // cw
-    some = max(1, chunks // 4)
+    some = max(1, 3 * chunks // 8)
     n_z = n_tp // 2
     bf, f32 = jnp.bfloat16, jnp.float32
     dma = pltpu.SemaphoreType.DMA

time: 38.9 us -> 38.3 us (0.985)
  Pallas kernels: 37 us -> 36.4 us
    pallas_call x1, Pallas kernels: 37 us -> 36.4 us  [per_device(): pl.pallas_call(functools.partial(kernel, n_ctx, n_tp), out_shape=jax.Shap...]
where the time goes in v8:
time: 38.3 us; the launch traced here: 38.1 us
  Pallas kernels  36.4 us (95%)
  local copies, waits for them, and re-layouts  1.67 us (4%)
    pallas_call x1, Pallas kernels, per_device(): pl.pallas_call(functools.partial(kernel, n_ctx, n_tp), out_shape=jax.Shap...  36.4 us
    unnamed x1, local copies, waits for them, and re-layouts  1.67 us

profile of v8, /device:TPU:26, one launch (start us, length us, event | category | flops | bytes accessed | tf_op | source)
XLA Modules:
  0.0 38.1 jit_solution(13427849892832464500)
XLA Ops:
  0.0 36.4 %conv_project.1 = bf16[1024,128]{1,0:T(8,128)(2,1)} custom-call(bf16[1024,128]{1,0:T(8,128)(2,1)} %q_hbm.1, bf16[1024,128]{1,0:T(8,128)(2,1)} %k_hbm.1, bf16[1024,128]{1,0:T(8,128)(2,1)} %v_hbm.1, bf16[1024,128]{1,0:T(8,128)(2,1)} %og_hbm.1, bf16[64,128]{1,0:T(8,128)(2,1)} %mr_ref.1, f32[16,64]{1,0:T(8,128)} %bitcast.2, f32[16,64]{1,0:T(8,128)} %bitcast.3, ...), custom_call_target="tpu_custom_call" | custom-call | tf_op jit(solution)/shard_map/conv_project/pallas_call | solution.py:526
  36.4 1.7 %copy.10 = bf16[1024,128]{1,0:T(8,128)(2,1)} copy(bf16[1024,128]{1,0:T(8,128)(2,1)} %conv_project.1) | data formatting | bytes 524288

commit v9 on v8

--- a/solution.py
+++ b/solution.py
@@ -312,7 +312,7 @@
             entered = dot(jnp.concatenate([high, low, high], axis=1), coef_ref[k], ((1,), (1,)))
             wide = (loc_ref[rows, :] + entered).astype(jnp.bfloat16)
             gated = og_ref[rows, :].astype(jnp.float32) * wide.astype(jnp.float32)
-            gt_ref[:, rows] = gated.T.astype(jnp.bfloat16)
+            gt_ref[:, rows] = gated.astype(jnp.bfloat16).T
 
     def y_copy(p, c):
         return pltpu.make_async_remote_copy(

time: 38.3 us -> 38.3 us (level)
  no operation moved by 1% of the time
where the time goes in v9:
time: 38.3 us; the launch traced here: 38 us
  Pallas kernels  36.4 us (95%)
  local copies, waits for them, and re-layouts  1.67 us (4%)
    pallas_call x1, Pallas kernels, per_device(): pl.pallas_call(functools.partial(kernel, n_ctx, n_tp), out_shape=jax.Shap...  36.4 us
    unnamed x1, local copies, waits for them, and re-layouts  1.67 us

profile of v9, /device:TPU:26, one launch (start us, length us, event | category | flops | bytes accessed | tf_op | source)
XLA Modules:
  0.0 38.0 jit_solution(18361121740674806842)
XLA Ops:
  0.0 36.4 %conv_project.1 = bf16[1024,128]{1,0:T(8,128)(2,1)} custom-call(bf16[1024,128]{1,0:T(8,128)(2,1)} %q_hbm.1, bf16[1024,128]{1,0:T(8,128)(2,1)} %k_hbm.1, bf16[1024,128]{1,0:T(8,128)(2,1)} %v_hbm.1, bf16[1024,128]{1,0:T(8,128)(2,1)} %og_hbm.1, bf16[64,128]{1,0:T(8,128)(2,1)} %mr_ref.1, f32[16,64]{1,0:T(8,128)} %bitcast.2, f32[16,64]{1,0:T(8,128)} %bitcast.3, ...), custom_call_target="tpu_custom_call" | custom-call | tf_op jit(solution)/shard_map/conv_project/pallas_call | solution.py:526
  36.4 1.7 %copy.10 = bf16[1024,128]{1,0:T(8,128)(2,1)} copy(bf16[1024,128]{1,0:T(8,128)(2,1)} %conv_project.1) | data formatting | bytes 524288
